TPU v7x, 128 devices: a whole 4x4x4 slice. The times are simulated.
128 devices in a mesh: section: 8 (over z, core), kfac: 16 (over y, x).
Axes of the slice: x: 4, y: 4, z: 4, core: 2. Of those that a mesh axis runs over, the one named last changes fastest.
Arguments:
- top_cotangent: bfloat16 [8, 32, 8192], P(None, None, 'kfac'), may hold values from -6 to 6
- inputs: bfloat16 [8, 8, 32, 8192], P('section'), may hold values from -6 to 6
- proj_weight: bfloat16 [8, 8192, 2048], P('section', None, 'kfac'), may hold values from -0.0625 to 0.0625
- return_weight: bfloat16 [8, 2048, 8192], P('section', 'kfac'), may hold values from -0.125 to 0.125
- owners: int32 [8, 8], P('section'), may hold values from 0 to 15, as said below
- input_inverses: bfloat16 [8, 16, 1024, 1024], P('section', 'kfac'), as said below
- output_inverses: bfloat16 [8, 2, 1024, 1024], P('section'), as said below
Outputs:
- section_cotangents: bfloat16 [8, 8, 32, 8192], P('section', None, None, 'kfac')
- preconditioned: bfloat16 [8, 8192, 2048], P('section', None, 'kfac')
Inputs may be any that keep to these rules, and one draw needn't show every extreme that they name: In each section's row no kfac device is named more than once (the eight blocks of a section have eight distinct owners). `input_inverses`: slot o + j of a section holds the inverse for the (j+1)-th block, in block order, that owners assigns to device o; slots that no block uses hold arbitrary values. Each block is symmetric. `output_inverses`: each block is symmetric.
All inputs are finite; a program needn't handle non-finite values.
Results may differ from a plain program's by a relative error of at most 0.035.
Values may be sent and summed in bfloat16 or wider, within the bound.
No kernel may reach another device: no remote copies, remote signals or barrier semaphores. Data moves between devices by JAX's collectives and lax.ppermute only.
A program may use at most 128 MiB of HBM per device.

v0:
```python
import jax
import jax.numpy as jnp
from jax import lax
from jax.experimental import pallas as pl
from jax.experimental.pallas import tpu as pltpu
from jax.sharding import PartitionSpec as P

BF = jnp.bfloat16
F32 = jnp.float32
SIDE = 4


def silu_slope(values):
    sigmoid = jax.nn.sigmoid(values)
    return sigmoid * (1.0 + values * (1.0 - sigmoid))


def slot_numbers(owner_row):
    blocks = owner_row.shape[0]
    earlier = jnp.arange(blocks)[None, :] < jnp.arange(blocks)[:, None]
    shared = owner_row[None, :] == owner_row[:, None]
    return jnp.sum(jnp.logical_and(earlier, shared).astype(jnp.int32), axis=1)


def permute_grid(block, source):
    route = []
    for row in range(SIDE):
        for col in range(SIDE):
            from_row, from_col = source(row, col)
            route.append((from_row * SIDE + from_col, row * SIDE + col))
    return lax.ppermute(block, "kfac", route)


def from_col(block, distance):
    return permute_grid(block, lambda row, col: (row, (col + distance) % SIDE))


def from_row(block, distance, core):
    size = SIDE * SIDE
    route = []
    for section in range(core, lax.axis_size("section"), 2):
        for row in range(SIDE):
            for col in range(SIDE):
                source = (row + distance) % SIDE * SIDE + col
                route.append((section * size + source, section * size + row * SIDE + col))
    return lax.ppermute(block, ("section", "kfac"), route)


def to_other_core(block, core):
    sections = range(core, lax.axis_size("section"), 2)
    return lax.ppermute(block, "section", [(i, i ^ 1) for i in sections])


def swap_cores(block):
    sections = lax.axis_size("section")
    return lax.ppermute(block, "section", [(i, i ^ 1) for i in range(sections)])


def pass_down(block):
    sections = lax.axis_size("section")
    return lax.ppermute(block, "section", [(i, i - 2) for i in range(2, sections)])


def sum_rows(block):
    near = permute_grid(block, lambda row, col: (row ^ 1, col))
    half = (block.astype(F32) + near.astype(F32)).astype(BF)
    far = permute_grid(half, lambda row, col: (SIDE - 1 - row, col))
    return half.astype(F32) + far.astype(F32)


def exchange(pieces, groups):
    return lax.all_to_all(pieces, "kfac", 0, 0, axis_index_groups=groups)


ROW_GROUPS = [[row * SIDE + col for col in range(SIDE)] for row in range(SIDE)]
COL_GROUPS = [[row * SIDE + col for row in range(SIDE)] for col in range(SIDE)]


def dot_nt(left, right):
    return lax.dot_general(left, right, (((1,), (1,)), ((), ())), preferred_element_type=F32)


def dot_nn(left, right):
    return lax.dot_general(left, right, (((1,), (0,)), ((), ())), preferred_element_type=F32)


def whole(count):
    return [pl.BlockSpec(memory_space=pltpu.VMEM)] * count


def chunk(index, size):
    return pl.ds(pl.multiple_of(lax.rem(index + SIDE, SIDE) * size, size), size)


def cut(row, returning, weight):
    stripe, width = returning.shape
    quarter = width // SIDE

    def body(row_ref, returning_ref, weight_ref, *outs):
        for j, out_ref in enumerate(outs):
            here = chunk(row_ref[0] - j, quarter)
            out_ref[:stripe, :] = returning_ref[:, here]
            out_ref[stripe:, :] = weight_ref[here, :].T

    return pl.pallas_call(
        body,
        in_specs=[pl.BlockSpec(memory_space=pltpu.SMEM)] + whole(2),
        out_specs=whole(SIDE),
        out_shape=[jax.ShapeDtypeStruct((2 * stripe, quarter), weight.dtype)] * SIDE,
        cost_estimate=pl.CostEstimate(
            flops=0, bytes_accessed=8 * stripe * width, transcendentals=0
        ),
    )(row[None], returning, weight)


def after(value, *others):
    return lax.optimization_barrier((value,) + others)[0]


def left_kernel(block_ref, factor_ref, x_ref, out_ref):
    out_ref[...] = dot_nt(factor_ref[...], x_ref[...]).astype(out_ref.dtype)


def left_product(block_here, factor, x):
    size = factor.shape[0]
    tokens = x.shape[0]
    return pl.pallas_call(
        left_kernel,
        grid_spec=pltpu.PrefetchScalarGridSpec(
            num_scalar_prefetch=1,
            grid=(1,),
            in_specs=[
                pl.BlockSpec((size, size), lambda i, block: (0, 0)),
                pl.BlockSpec((tokens, size), lambda i, block: (0, block[0])),
            ],
            out_specs=pl.BlockSpec((size, tokens), lambda i, block: (0, 0)),
        ),
        out_shape=jax.ShapeDtypeStruct((size, tokens), BF),
        cost_estimate=pl.CostEstimate(
            flops=2 * size * size * tokens,
            bytes_accessed=2 * size * (size + 2 * tokens),
            transcendentals=0,
        ),
    )(block_here, factor, x)


def spread_kernel(slots_ref, *refs):
    lefts, right_ref, out_ref = refs[:SIDE], refs[SIDE], refs[SIDE + 1]
    size = lefts[0].shape[0]
    for i, left_ref in enumerate(lefts):
        product = dot_nn(left_ref[...], right_ref[...])
        out_ref[i * size : (i + 1) * size, :] = product.astype(out_ref.dtype)


def spread(slots, left, right, height):
    depth = left.shape[1]
    width = right.shape[1]
    block_count = slots.shape[0]
    streams = [
        pl.BlockSpec(
            (height // 2, depth), lambda b, slots, i=i: (slots[2 * b + i // 2] * 2 + i % 2, 0)
        )
        for i in range(SIDE)
    ]
    return pl.pallas_call(
        spread_kernel,
        grid_spec=pltpu.PrefetchScalarGridSpec(
            num_scalar_prefetch=1,
            grid=(block_count // 2,),
            in_specs=streams + [pl.BlockSpec((depth, width), lambda b, slots: (0, 0))],
            out_specs=pl.BlockSpec((2 * height, width), lambda b, slots: (b, 0)),
        ),
        out_shape=jax.ShapeDtypeStruct((block_count * height, width), BF),
        cost_estimate=pl.CostEstimate(
            flops=2 * block_count * height * depth * width,
            bytes_accessed=2 * block_count * height * (depth + width),
            transcendentals=0,
        ),
    )(slots, *[left] * SIDE, right)


def join(own, ahead, far, behind):
    size, width = own.shape
    joined = jnp.zeros((SIDE * size, width), own.dtype)
    starts = (0, size, 3 * size, 2 * size, 2 * size + size // 2)
    for part, start in zip((own, ahead, behind) + tuple(far), starts):
        joined = lax.dynamic_update_slice(joined, part, (start, 0))
    return joined


def on_device(
    top_cotangent, inputs, proj_weight, return_weight, owners, input_inverses, output_inverses
):
    section_count = lax.axis_size("section")
    section_here = lax.axis_index("section")
    kfac_here = lax.axis_index("kfac")
    row, col = kfac_here // SIDE, kfac_here % SIDE
    core, plane = section_here % 2, section_here // 2
    odd_here = core == 1
    micro, per_micro, shard_width = top_cotangent.shape
    tokens = micro * per_micro
    group_tokens = tokens // SIDE
    x = inputs[0].reshape(tokens, -1)
    weight = proj_weight[0]
    width, stripe = weight.shape
    quarter = width // SIDE
    pair = SIDE // 2
    block_width = input_inverses.shape[2]
    block_count = width // block_width

    top = exchange(top_cotangent.reshape(SIDE, group_tokens, shard_width), ROW_GROUPS)

    slopes = silu_slope(dot_nn(x, weight)).astype(BF).reshape(1, SIDE, group_tokens, stripe)
    slopes = jnp.broadcast_to(slopes, (SIDE, SIDE, group_tokens, stripe))
    slopes = lax.all_to_all(slopes.reshape(SIDE * SIDE, group_tokens, stripe), "kfac", 0, 0)

    def odd_even(kept, received):
        return jnp.where(odd_here, kept, received), jnp.where(odd_here, received, kept)

    def in_ring_order(by_col):
        twice = jnp.concatenate([by_col, by_col], axis=1)
        return lax.dynamic_slice_in_dim(twice, col, SIDE, 1)

    def chain_factors(slopes):
        slopes = slopes.reshape(SIDE, SIDE, group_tokens, stripe)
        kept = lax.dynamic_slice_in_dim(slopes, pair * core, pair, 0)
        sent = lax.dynamic_slice_in_dim(slopes, pair * (1 - core), pair, 0)
        return [
            jnp.transpose(in_ring_order(part), (2, 1, 0, 3)).reshape(group_tokens, -1)
            for part in odd_even(kept, swap_cores(sent))
        ]

    pieces = cut(row, return_weight[0], weight)
    picks = [lax.rem(place - row + SIDE, SIDE) for place in range(SIDE)]

    def exchange_rows(core_now, first, last, *held):
        own = [after(piece, *held)[first:last] for piece in pieces]
        return own[:1] + [from_row(own[j], j, core_now) for j in range(1, SIDE)]

    def core_groups(rows, core_now, *gate):
        rows = [after(rows[0], *gate)] + rows[1:]
        groups = [
            jnp.concatenate([lax.select_n(p, *rows) for p in picks[i : i + pair]])
            for i in range(0, SIDE, pair)
        ]
        return groups[core_now], to_other_core(groups[1 - core_now], core_now)

    half = stripe
    odd = exchange_rows(1, 0, 2 * stripe)
    kept, received = core_groups([part[:stripe] for part in odd], 1, top, slopes)
    block = jnp.where(core == 1, kept, received)
    ahead, behind = from_col(block, 1), from_col(block, SIDE - 1)
    kept, received = core_groups([part[stripe:] for part in odd], 1, block)
    even = exchange_rows(0, 0, 2 * stripe, *odd[1:])
    before = even[1:]
    sent = []
    gathered = []
    for core_now in (1, 0, 0, None):
        back_half = (ahead[:half], behind[half:])
        last, near = block, (ahead, behind)
        if core_now is None:
            far = (from_col(back_half[0], 1), from_col(back_half[1], SIDE - 1))
        else:
            block = jnp.where(core == core_now, after(kept, ahead, behind, *before), received)
            sent.append([jnp.concatenate([part, block]) for part in back_half])
            ahead, behind = from_col(sent[-1][0], 1), from_col(sent[-1][1], SIDE - 1)
            before = []
            if len(sent) == 1:
                before = factors = chain_factors(after(slopes, *sent[0]))
            far = (ahead[:half], behind[:half])
            ahead, behind = ahead[half:], behind[half:]
            if len(gathered) < 2:
                kind = len(gathered) * stripe
                rows = [part[kind : kind + stripe] for part in even]
                kept, received = core_groups(rows, 0, block)
        gathered.append(join(last, near[0], far, near[1]))
    back_odd, proj_odd, back_even, proj_even = gathered
    chain_weights = ((back_odd, proj_odd), (back_even, proj_even))

    top = top.reshape(SIDE, group_tokens, shard_width)
    shard = jnp.concatenate([top[i] for i in range(SIDE)], axis=1)

    group_here = row // pair
    out_rows = lax.dynamic_slice(
        output_inverses[0],
        (group_here, 0, row % pair * SIDE * stripe),
        (1, block_width, SIDE * stripe),
    ).reshape(pair, SIDE, stripe, SIDE * stripe)
    out_rows = jnp.swapaxes(in_ring_order(out_rows), 0, 1).reshape(block_width, SIDE * stripe)

    targets = owners[0] + slot_numbers(owners[0])
    mine = targets == kfac_here
    block_here = jnp.sum(jnp.where(mine, jnp.arange(block_count, dtype=jnp.int32), 0))
    left_here = left_product(block_here[None], input_inverses[0, 0], x)

    saved = None
    for visit in range(section_count // 2):
        new = []
        for factor, (back_now, proj_now) in zip(factors, chain_weights):
            if visit == 0:
                shard = after(shard, left_here) if new else after(shard, *sent[1])
            back = sum_rows(dot_nt(shard, back_now).astype(BF))
            slope = (back * factor).astype(BF)
            if visit == 0 and not new:
                slope = after(slope, *sent[2])
            own = dot_nn(slope, proj_now)
            summed = shard.astype(F32) + own + swap_cores(own.astype(BF)).astype(F32)
            shard = summed.astype(BF)
            new += [slope, shard]
        active = plane == section_count // 2 - 1 - visit
        saved = new if saved is None else [jnp.where(active, n, o) for n, o in zip(new, saved)]
        if visit == 0:
            left_all = lax.all_gather(after(left_here, shard), "kfac", axis=0, tiled=True)
        if visit < section_count // 2 - 1:
            shard = pass_down(shard)

    slope_odd, shard_odd, slope_even, shard_even = saved
    slope_mine = jnp.where(odd_here, slope_odd, slope_even)
    slope_other = swap_cores(jnp.where(odd_here, slope_even, slope_odd))
    slope_group = jnp.where(core == group_here, slope_mine, slope_other)
    right = dot_nn(slope_group, out_rows).astype(BF).reshape(group_tokens, SIDE, stripe)
    output = jnp.where(odd_here, shard_odd, shard_even).reshape(group_tokens, SIDE, shard_width)
    both = jnp.swapaxes(jnp.concatenate([output, right], axis=2), 0, 1)
    both = exchange(both, ROW_GROUPS).reshape(tokens, shard_width + stripe)
    outputs, right = both[:, :shard_width], both[:, shard_width:]
    result = spread(targets, left_all, right, block_width)
    return outputs.reshape(1, micro, per_micro, shard_width), result[None]


def solution(mesh):
    return jax.shard_map(
        on_device,
        mesh=mesh,
        in_specs=(
            P(None, None, "kfac"),
            P("section", None, None, None),
            P("section", None, "kfac"),
            P("section", "kfac", None),
            P("section", None),
            P("section", "kfac", None, None),
            P("section", None, None, None),
        ),
        out_specs=(P("section", None, None, "kfac"), P("section", None, "kfac")),
        check_vma=False,
    )
```

profile of v0, /device:TPU:0, one launch (start us, length us, event | category | flops | bytes accessed | tf_op | source)
XLA Modules:
  0.0 401.9 jit_solution(2918408200138260955)
XLA Ops:
  28.0 5.2 %all-to-all-start.1 = ((bf16[16,64,128]{2,1,0:T(8,128)(2,1)}), bf16[16,64,128]{2,1,0:T(8,128)(2,1)}, u32[]{:S(2)}, u32[]{:S(2)}) async-start(bf16[16,64,128]{2,1,0:T(8,128)(2,1)} %bitcast.10), calls=%async_computation.1 | async-start | bytes 524288 | tf_op jit(solution)/shard_map/all_to_all | solution.py:215
  33.6 8.6 %all-to-all-done.1 = bf16[16,64,128]{2,1,0:T(8,128)(2,1)} async-done(((bf16[16,64,128]{2,1,0:T(8,128)(2,1)}), bf16[16,64,128]{2,1,0:T(8,128)(2,1)}, u32[]{:S(2)}, u32[]{:S(2)}) %all-to-all-start.1) | async-done | bytes 262176 | tf_op jit(solution)/shard_map/all_to_all | solution.py:215
  74.9 9.2 %collective-permute-done.8 = bf16[256,2048]{1,0:T(8,128)(2,1)S(1)} collective-permute-done((bf16[256,2048]{1,0:T(8,128)(2,1)}, bf16[256,2048]{1,0:T(8,128)(2,1)S(1)}, u32[]{:S(2)}, u32[]{:S(2)}) %collective-permute-start.8) | collective-permute-done | bytes 1048608 | tf_op jit(solution)/shard_map/ppermute | solution.py:46
  112.4 14.1 %collective-permute-done.10 = bf16[384,2048]{1,0:T(8,128)(2,1)} collective-permute-done((bf16[384,2048]{1,0:T(8,128)(2,1)}, bf16[384,2048]{1,0:T(8,128)(2,1)}, u32[]{:S(2)}, u32[]{:S(2)}) %collective-permute-start.10) | collective-permute-done | bytes 1572896 | tf_op jit(solution)/shard_map/ppermute | solution.py:31
  137.0 5.0 %collective-permute-start.14 = (bf16[64,1024]{1,0:T(8,128)(2,1)S(1)}, bf16[64,1024]{1,0:T(8,128)(2,1)S(1)}, u32[]{:S(2)}, u32[]{:S(2)}) collective-permute-start(bf16[64,1024]{1,0:T(8,128)(2,1)S(1)} %convolution_convert_fusion.7), channel_id=1, source_target_pairs={{4,0},{5,1},{6,2},{7,3},{0,4},{1,5},{2,6},{3,7},{12,8},{13,9},{14,... | collective-permute-start | bytes 393224 | tf_op jit(solution)/shard_map/ppermute | solution.py:31
  152.0 12.8 %collective-permute-done.16 = bf16[384,2048]{1,0:T(8,128)(2,1)S(1)} collective-permute-done((bf16[384,2048]{1,0:T(8,128)(2,1)S(1)}, bf16[384,2048]{1,0:T(8,128)(2,1)S(1)}, u32[]{:S(2)}, u32[]{:S(2)}) %collective-permute-start.16) | collective-permute-done | bytes 1572896 | tf_op jit(solution)/shard_map/ppermute | solution.py:31
  170.0 29.8 %collective-permute-done.20 = bf16[384,2048]{1,0:T(8,128)(2,1)S(1)} collective-permute-done((bf16[384,2048]{1,0:T(8,128)(2,1)S(1)}, bf16[384,2048]{1,0:T(8,128)(2,1)S(1)}, u32[]{:S(2)}, u32[]{:S(2)}) %collective-permute-start.20) | collective-permute-done | bytes 1572896 | tf_op jit(solution)/shard_map/ppermute | solution.py:31
  203.5 7.2 %collective-permute-start.22 = (bf16[64,1024]{1,0:T(8,128)(2,1)S(1)}, bf16[64,1024]{1,0:T(8,128)(2,1)S(1)}, u32[]{:S(2)}, u32[]{:S(2)}) collective-permute-start(bf16[64,1024]{1,0:T(8,128)(2,1)S(1)} %convolution_convert_fusion.6), channel_id=1, source_target_pairs={{4,0},{5,1},{6,2},{7,3},{0,4},{1,5},{2,6},{3,7},{12,8},{13,9},{14,... | collective-permute-start | bytes 393224 | tf_op jit(solution)/shard_map/ppermute | solution.py:31
  224.2 9.2 %collective-permute-done.27 = bf16[64,2048]{1,0:T(8,128)(2,1)S(1)} collective-permute-done((bf16[64,2048]{1,0:T(8,128)(2,1)S(1)}, bf16[64,2048]{1,0:T(8,128)(2,1)S(1)}, u32[]{:S(2)}, u32[]{:S(2)}) %collective-permute-start.27) | collective-permute-done | bytes 262176 | tf_op jit(solution)/shard_map/ppermute | solution.py:61
  237.9 7.0 %collective-permute-done.28 = bf16[64,1024]{1,0:T(8,128)(2,1)S(1)} collective-permute-done((bf16[64,1024]{1,0:T(8,128)(2,1)S(1)}, bf16[64,1024]{1,0:T(8,128)(2,1)S(1)}, u32[]{:S(2)}, u32[]{:S(2)}) %collective-permute-start.28) | collective-permute-done | bytes 131104 | tf_op jit(solution)/shard_map/ppermute | solution.py:31
  255.2 10.0 %collective-permute-start.31 = (bf16[64,1024]{1,0:T(8,128)(2,1)S(1)}, bf16[64,1024]{1,0:T(8,128)(2,1)S(1)}, u32[]{:S(2)}, u32[]{:S(2)}) collective-permute-start(bf16[64,1024]{1,0:T(8,128)(2,1)S(1)} %convolution_convert_fusion.4), channel_id=1, source_target_pairs={{4,0},{5,1},{6,2},{7,3},{0,4},{1,5},{2,6},{3,7},{12,8},{13,9},{14,... | collective-permute-start | bytes 393224 | tf_op jit(solution)/shard_map/ppermute | solution.py:31
  265.2 8.8 %collective-permute-done.31 = bf16[64,1024]{1,0:T(8,128)(2,1)S(1)} collective-permute-done((bf16[64,1024]{1,0:T(8,128)(2,1)S(1)}, bf16[64,1024]{1,0:T(8,128)(2,1)S(1)}, u32[]{:S(2)}, u32[]{:S(2)}) %collective-permute-start.31) | collective-permute-done | bytes 131104 | tf_op jit(solution)/shard_map/ppermute | solution.py:31
  275.9 8.1 %collective-permute-done.32 = bf16[64,1024]{1,0:T(8,128)(2,1)S(1)} collective-permute-done((bf16[64,1024]{1,0:T(8,128)(2,1)S(1)}, bf16[64,1024]{1,0:T(8,128)(2,1)S(1)}, u32[]{:S(2)}, u32[]{:S(2)}) %collective-permute-start.32) | collective-permute-done | bytes 131104 | tf_op jit(solution)/shard_map/ppermute | solution.py:31
  287.9 9.4 %collective-permute-done.34 = bf16[64,2048]{1,0:T(8,128)(2,1)S(1)} collective-permute-done((bf16[64,2048]{1,0:T(8,128)(2,1)S(1)}, bf16[64,2048]{1,0:T(8,128)(2,1)S(1)}, u32[]{:S(2)}, u32[]{:S(2)}) %collective-permute-start.34) | collective-permute-done | bytes 262176 | tf_op jit(solution)/shard_map/ppermute | solution.py:61
  301.0 5.0 %collective-permute-done.35 = bf16[64,1024]{1,0:T(8,128)(2,1)S(1)} collective-permute-done((bf16[64,1024]{1,0:T(8,128)(2,1)S(1)}, bf16[64,1024]{1,0:T(8,128)(2,1)S(1)}, u32[]{:S(2)}, u32[]{:S(2)}) %collective-permute-start.35) | collective-permute-done | bytes 131104 | tf_op jit(solution)/shard_map/ppermute | solution.py:31
  307.3 5.0 %collective-permute-done.36 = bf16[64,1024]{1,0:T(8,128)(2,1)S(1)} collective-permute-done((bf16[64,1024]{1,0:T(8,128)(2,1)S(1)}, bf16[64,1024]{1,0:T(8,128)(2,1)S(1)}, u32[]{:S(2)}, u32[]{:S(2)}) %collective-permute-start.36) | collective-permute-done | bytes 131104 | tf_op jit(solution)/shard_map/ppermute | solution.py:31
  316.4 5.5 %collective-permute-done.38 = bf16[64,1024]{1,0:T(8,128)(2,1)S(1)} collective-permute-done((bf16[64,1024]{1,0:T(8,128)(2,1)S(1)}, bf16[64,1024]{1,0:T(8,128)(2,1)S(1)}, u32[]{:S(2)}, u32[]{:S(2)}) %collective-permute-start.38) | collective-permute-done | bytes 131104 | tf_op jit(solution)/shard_map/ppermute | solution.py:31
  323.2 5.0 %collective-permute-done.39 = bf16[64,1024]{1,0:T(8,128)(2,1)S(1)} collective-permute-done((bf16[64,1024]{1,0:T(8,128)(2,1)S(1)}, bf16[64,1024]{1,0:T(8,128)(2,1)S(1)}, u32[]{:S(2)}, u32[]{:S(2)}) %collective-permute-start.39) | collective-permute-done | bytes 131104 | tf_op jit(solution)/shard_map/ppermute | solution.py:31
  332.1 8.9 %collective-permute-done.41 = bf16[64,2048]{1,0:T(8,128)(2,1)S(1)} collective-permute-done((bf16[64,2048]{1,0:T(8,128)(2,1)S(1)}, bf16[64,2048]{1,0:T(8,128)(2,1)S(1)}, u32[]{:S(2)}, u32[]{:S(2)}) %collective-permute-start.41) | collective-permute-done | bytes 262176 | tf_op jit(solution)/shard_map/ppermute | solution.py:61
  344.7 5.0 %collective-permute-done.42 = bf16[64,1024]{1,0:T(8,128)(2,1)S(1)} collective-permute-done((bf16[64,1024]{1,0:T(8,128)(2,1)S(1)}, bf16[64,1024]{1,0:T(8,128)(2,1)S(1)}, u32[]{:S(2)}, u32[]{:S(2)}) %collective-permute-start.42) | collective-permute-done | bytes 131104 | tf_op jit(solution)/shard_map/ppermute | solution.py:31
  351.0 5.0 %collective-permute-done.43 = bf16[64,1024]{1,0:T(8,128)(2,1)S(1)} collective-permute-done((bf16[64,1024]{1,0:T(8,128)(2,1)S(1)}, bf16[64,1024]{1,0:T(8,128)(2,1)S(1)}, u32[]{:S(2)}, u32[]{:S(2)}) %collective-permute-start.43) | collective-permute-done | bytes 131104 | tf_op jit(solution)/shard_map/ppermute | solution.py:31
  360.1 5.6 %collective-permute-done.45 = bf16[64,1024]{1,0:T(8,128)(2,1)} collective-permute-done((bf16[64,1024]{1,0:T(8,128)(2,1)S(1)}, bf16[64,1024]{1,0:T(8,128)(2,1)}, u32[]{:S(2)}, u32[]{:S(2)}) %collective-permute-start.45) | collective-permute-done | bytes 131104 | tf_op jit(solution)/shard_map/ppermute | solution.py:31
  377.3 10.6 %all_to_all.15 = bf16[4,64,640]{2,1,0:T(8,128)(2,1)S(1)} all-to-all(bf16[4,64,640]{2,1,0:T(8,128)(2,1)S(1)} %maximum_bitcast_fusion), channel_id=1, replica_groups={{0,1,2,3},{4,5,6,7},{8,9,10,11},{12,13,14,15},{16,17,18,19},{20,21,22,2..., dimensions={0} | all-to-all | bytes 655360 | tf_op jit(solution)/shard_map/all_to_all | solution.py:72
  389.2 5.6 %shard_map.88 = bf16[8192,128]{1,0:T(8,128)(2,1)} custom-call(s32[8]{0:T(128)} %get-tuple-element.46.slots_ref, bf16[16384,256]{1,0:T(8,128)(2,1)} %all-gather.2.cloned.1.call-done.refs_0_.refs_1_.refs_2_.refs_3_, bf16[16384,256]{1,0:T(8,128)(2,1)} %all-gather.2.cloned.1.call-done.refs_0_.refs_1_.refs_2_.refs_3_, ...), custom_call_target="tpu_custom_call" | custom-call | flops 536870912 | bytes 6291456 | tf_op jit(solution)/shard_map/pallas_call | solution.py:165
  (227 shorter events, 180.9 us)
Async XLA Ops:
  12.0 30.2 %collective-permute-start.2 = (bf16[256,2048]{1,0:T(8,128)(2,1)}, bf16[256,2048]{1,0:T(8,128)(2,1)S(1)}, u32[]{:S(2)}, u32[]{:S(2)}) collective-permute-start(bf16[256,2048]{1,0:T(8,128)(2,1)} %get-tuple-element.30), channel_id=1, source_target_pairs={{28,16},{29,17},{30,18},{31,19},{16,20},{17,21},{18,22},{19,23},{2... | collective-permute-start | bytes 3145736 | tf_op jit(solution)/shard_map/ppermute | solution.py:46
  12.8 29.4 %collective-permute-start.1 = (bf16[256,2048]{1,0:T(8,128)(2,1)}, bf16[256,2048]{1,0:T(8,128)(2,1)}, u32[]{:S(2)}, u32[]{:S(2)}) collective-permute-start(bf16[256,2048]{1,0:T(8,128)(2,1)} %get-tuple-element.29), channel_id=1, source_target_pairs={{24,16},{25,17},{26,18},{27,19},{28,20},{29,21},{30,22},{31,23},{1... | collective-permute-start | bytes 3145736 | tf_op jit(solution)/shard_map/ppermute | solution.py:46
  14.5 27.7 %collective-permute-start = (bf16[256,2048]{1,0:T(8,128)(2,1)}, bf16[256,2048]{1,0:T(8,128)(2,1)}, u32[]{:S(2)}, u32[]{:S(2)}) collective-permute-start(bf16[256,2048]{1,0:T(8,128)(2,1)} %get-tuple-element.28), channel_id=1, source_target_pairs={{20,16},{21,17},{22,18},{23,19},{24,20},{25,21},{26,22},{27,23},{2... | collective-permute-start | bytes 3145736 | tf_op jit(solution)/shard_map/ppermute | solution.py:46
  16.2 11.1 %all-to-all-start = ((bf16[4,64,512]{2,1,0:T(8,128)(2,1)}), bf16[4,64,512]{2,1,0:T(8,128)(2,1)S(1)}, u32[]{:S(2)}, u32[]{:S(2)}) async-start(bf16[4,64,512]{2,1,0:T(8,128)(2,1)} %bitcast), calls=%async_computation | async-start | bytes 524288 | tf_op jit(solution)/shard_map/all_to_all | solution.py:72
  28.0 14.2 %all-to-all-start.1 = ((bf16[16,64,128]{2,1,0:T(8,128)(2,1)}), bf16[16,64,128]{2,1,0:T(8,128)(2,1)}, u32[]{:S(2)}, u32[]{:S(2)}) async-start(bf16[16,64,128]{2,1,0:T(8,128)(2,1)} %bitcast.10), calls=%async_computation.1 | async-start | bytes 524288 | tf_op jit(solution)/shard_map/all_to_all | solution.py:215
  33.2 356.0 %all-gather.2.cloned.1.call-start = ((), (), s32[]{:S(2)}) async-start(), calls=%async_computation.3 | async-start | bytes 8912896 | tf_op jit(solution)/shard_map/all_gather | solution.py:313
  45.4 17.8 %collective-permute-start.3 = (bf16[256,2048]{1,0:T(8,128)(2,1)}, bf16[256,2048]{1,0:T(8,128)(2,1)}, u32[]{:S(2)}, u32[]{:S(2)}) collective-permute-start(bf16[256,2048]{1,0:T(8,128)(2,1)} %pad_maximum_fusion.6), channel_id=1, source_target_pairs={{16,0},{48,32},{80,64},{112,96},{17,1},{49,33},{81,65},{113,97},{1... | collective-permute-start | bytes 3145736 | tf_op jit(solution)/shard_map/ppermute | solution.py:51
  51.8 17.7 %collective-permute-start.6 = (bf16[256,2048]{1,0:T(8,128)(2,1)}, bf16[256,2048]{1,0:T(8,128)(2,1)S(1)}, u32[]{:S(2)}, u32[]{:S(2)}) collective-permute-start(bf16[256,2048]{1,0:T(8,128)(2,1)} %get-tuple-element.28), channel_id=1, source_target_pairs={{4,0},{5,1},{6,2},{7,3},{8,4},{9,5},{10,6},{11,7},{12,8},{13,9},{1... | collective-permute-start | bytes 3145736 | tf_op jit(solution)/shard_map/ppermute | solution.py:46
  54.4 20.4 %collective-permute-start.7 = (bf16[256,2048]{1,0:T(8,128)(2,1)}, bf16[256,2048]{1,0:T(8,128)(2,1)S(1)}, u32[]{:S(2)}, u32[]{:S(2)}) collective-permute-start(bf16[256,2048]{1,0:T(8,128)(2,1)} %get-tuple-element.29), channel_id=1, source_target_pairs={{8,0},{9,1},{10,2},{11,3},{12,4},{13,5},{14,6},{15,7},{0,8},{1,9},... | collective-permute-start | bytes 3145736 | tf_op jit(solution)/shard_map/ppermute | solution.py:46
  58.6 25.5 %collective-permute-start.8 = (bf16[256,2048]{1,0:T(8,128)(2,1)}, bf16[256,2048]{1,0:T(8,128)(2,1)S(1)}, u32[]{:S(2)}, u32[]{:S(2)}) collective-permute-start(bf16[256,2048]{1,0:T(8,128)(2,1)} %get-tuple-element.30), channel_id=1, source_target_pairs={{12,0},{13,1},{14,2},{15,3},{0,4},{1,5},{2,6},{3,7},{4,8},{5,9},{6... | collective-permute-start | bytes 3145736 | tf_op jit(solution)/shard_map/ppermute | solution.py:46
  65.0 21.7 %collective-permute-start.4 = (bf16[256,2048]{1,0:T(8,128)(2,1)S(1)}, bf16[256,2048]{1,0:T(8,128)(2,1)S(1)}, u32[]{:S(2)}, u32[]{:S(2)}) collective-permute-start(bf16[256,2048]{1,0:T(8,128)(2,1)S(1)} %maximum_select_fusion), channel_id=1, source_target_pairs={{1,0},{2,1},{3,2},{0,3},{5,4},{6,5},{7,6},{4,7},{9,8},{10,9},{11,1... | collective-permute-start | bytes 3145736 | tf_op jit(solution)/shard_map/ppermute | solution.py:31
  68.0 22.1 %collective-permute-start.5 = (bf16[256,2048]{1,0:T(8,128)(2,1)S(1)}, bf16[256,2048]{1,0:T(8,128)(2,1)S(1)}, u32[]{:S(2)}, u32[]{:S(2)}) collective-permute-start(bf16[256,2048]{1,0:T(8,128)(2,1)S(1)} %maximum_select_fusion), channel_id=1, source_target_pairs={{3,0},{0,1},{1,2},{2,3},{7,4},{4,5},{5,6},{6,7},{11,8},{8,9},{9,10... | collective-permute-start | bytes 3145736 | tf_op jit(solution)/shard_map/ppermute | solution.py:31
  69.5 20.6 %collective-permute-start.9 = (bf16[256,2048]{1,0:T(8,128)(2,1)S(1)}, bf16[256,2048]{1,0:T(8,128)(2,1)S(1)}, u32[]{:S(2)}, u32[]{:S(2)}) collective-permute-start(bf16[256,2048]{1,0:T(8,128)(2,1)S(1)} %pad_maximum_fusion.8), channel_id=1, source_target_pairs={{16,0},{48,32},{80,64},{112,96},{17,1},{49,33},{81,65},{113,97},{1... | collective-permute-start | bytes 3145736 | tf_op jit(solution)/shard_map/ppermute | solution.py:51
  95.0 31.5 %collective-permute-start.10 = (bf16[384,2048]{1,0:T(8,128)(2,1)}, bf16[384,2048]{1,0:T(8,128)(2,1)}, u32[]{:S(2)}, u32[]{:S(2)}) collective-permute-start(bf16[384,2048]{1,0:T(8,128)(2,1)} %get-tuple-element.78), channel_id=1, source_target_pairs={{1,0},{2,1},{3,2},{0,3},{5,4},{6,5},{7,6},{4,7},{9,8},{10,9},{11,1... | collective-permute-start | bytes 4718600 | tf_op jit(solution)/shard_map/ppermute | solution.py:31
  95.3 33.3 %collective-permute-start.11 = (bf16[384,2048]{1,0:T(8,128)(2,1)}, bf16[384,2048]{1,0:T(8,128)(2,1)}, u32[]{:S(2)}, u32[]{:S(2)}) collective-permute-start(bf16[384,2048]{1,0:T(8,128)(2,1)} %get-tuple-element.77), channel_id=1, source_target_pairs={{3,0},{0,1},{1,2},{2,3},{7,4},{4,5},{5,6},{6,7},{11,8},{8,9},{9,10... | collective-permute-start | bytes 4718600 | tf_op jit(solution)/shard_map/ppermute | solution.py:31
  111.1 40.3 %collective-permute-start.18 = (bf16[256,2048]{1,0:T(8,128)(2,1)S(1)}, bf16[256,2048]{1,0:T(8,128)(2,1)S(1)}, u32[]{:S(2)}, u32[]{:S(2)}) collective-permute-start(bf16[256,2048]{1,0:T(8,128)(2,1)S(1)} %pad_maximum_fusion.12), channel_id=1, source_target_pairs={{0,16},{32,48},{64,80},{96,112},{1,17},{33,49},{65,81},{97,113},{2... | collective-permute-start | bytes 3145736 | tf_op jit(solution)/shard_map/ppermute | solution.py:51
  131.1 33.7 %collective-permute-start.16 = (bf16[384,2048]{1,0:T(8,128)(2,1)S(1)}, bf16[384,2048]{1,0:T(8,128)(2,1)S(1)}, u32[]{:S(2)}, u32[]{:S(2)}) collective-permute-start(bf16[384,2048]{1,0:T(8,128)(2,1)S(1)} %get-tuple-element.76), channel_id=1, source_target_pairs={{1,0},{2,1},{3,2},{0,3},{5,4},{6,5},{7,6},{4,7},{9,8},{10,9},{11,1... | collective-permute-start | bytes 4718600 | tf_op jit(solution)/shard_map/ppermute | solution.py:31
  132.9 31.9 %collective-permute-start.17 = (bf16[384,2048]{1,0:T(8,128)(2,1)S(1)}, bf16[384,2048]{1,0:T(8,128)(2,1)S(1)}, u32[]{:S(2)}, u32[]{:S(2)}) collective-permute-start(bf16[384,2048]{1,0:T(8,128)(2,1)S(1)} %get-tuple-element.75), channel_id=1, source_target_pairs={{3,0},{0,1},{1,2},{2,3},{7,4},{4,5},{5,6},{6,7},{11,8},{8,9},{9,10... | collective-permute-start | bytes 4718600 | tf_op jit(solution)/shard_map/ppermute | solution.py:31
  165.3 34.5 %collective-permute-start.20 = (bf16[384,2048]{1,0:T(8,128)(2,1)S(1)}, bf16[384,2048]{1,0:T(8,128)(2,1)S(1)}, u32[]{:S(2)}, u32[]{:S(2)}) collective-permute-start(bf16[384,2048]{1,0:T(8,128)(2,1)S(1)} %get-tuple-element.72), channel_id=1, source_target_pairs={{1,0},{2,1},{3,2},{0,3},{5,4},{6,5},{7,6},{4,7},{9,8},{10,9},{11,1... | collective-permute-start | bytes 4718600 | tf_op jit(solution)/shard_map/ppermute | solution.py:31
  166.8 34.6 %collective-permute-start.21 = (bf16[384,2048]{1,0:T(8,128)(2,1)S(1)}, bf16[384,2048]{1,0:T(8,128)(2,1)S(1)}, u32[]{:S(2)}, u32[]{:S(2)}) collective-permute-start(bf16[384,2048]{1,0:T(8,128)(2,1)S(1)} %get-tuple-element.71), channel_id=1, source_target_pairs={{3,0},{0,1},{1,2},{2,3},{7,4},{4,5},{5,6},{6,7},{11,8},{8,9},{9,10... | collective-permute-start | bytes 4718600 | tf_op jit(solution)/shard_map/ppermute | solution.py:31
  199.9 15.3 %collective-permute-start.24 = (bf16[128,2048]{1,0:T(8,128)(2,1)S(1)}, bf16[128,2048]{1,0:T(8,128)(2,1)S(1)}, u32[]{:S(2)}, u32[]{:S(2)}) collective-permute-start(bf16[128,2048]{1,0:T(8,128)(2,1)S(1)} %get-tuple-element.62), channel_id=1, source_target_pairs={{1,0},{2,1},{3,2},{0,3},{5,4},{6,5},{7,6},{4,7},{9,8},{10,9},{11,1... | collective-permute-start | bytes 1572872 | tf_op jit(solution)/shard_map/ppermute | solution.py:31
  201.4 13.7 %collective-permute-start.25 = (bf16[128,2048]{1,0:T(8,128)(2,1)S(1)}, bf16[128,2048]{1,0:T(8,128)(2,1)S(1)}, u32[]{:S(2)}, u32[]{:S(2)}) collective-permute-start(bf16[128,2048]{1,0:T(8,128)(2,1)S(1)} %get-tuple-element.60), channel_id=1, source_target_pairs={{3,0},{0,1},{1,2},{2,3},{7,4},{4,5},{5,6},{6,7},{11,8},{8,9},{9,10... | collective-permute-start | bytes 1572872 | tf_op jit(solution)/shard_map/ppermute | solution.py:31
  222.6 10.7 %collective-permute-start.27 = (bf16[64,2048]{1,0:T(8,128)(2,1)S(1)}, bf16[64,2048]{1,0:T(8,128)(2,1)S(1)}, u32[]{:S(2)}, u32[]{:S(2)}) collective-permute-start(bf16[64,2048]{1,0:T(8,128)(2,1)S(1)} %add_convert_fusion.6), channel_id=1, source_target_pairs={{32,0},{48,16},{64,32},{80,48},{96,64},{112,80},{33,1},{49,17},{65... | collective-permute-start | bytes 786440 | tf_op jit(solution)/shard_map/ppermute | solution.py:61
  255.2 18.9 %collective-permute-start.31 = (bf16[64,1024]{1,0:T(8,128)(2,1)S(1)}, bf16[64,1024]{1,0:T(8,128)(2,1)S(1)}, u32[]{:S(2)}, u32[]{:S(2)}) collective-permute-start(bf16[64,1024]{1,0:T(8,128)(2,1)S(1)} %convolution_convert_fusion.4), channel_id=1, source_target_pairs={{4,0},{5,1},{6,2},{7,3},{0,4},{1,5},{2,6},{3,7},{12,8},{13,9},{14,... | collective-permute-start | bytes 393224 | tf_op jit(solution)/shard_map/ppermute | solution.py:31
  (48 other events, 438.9 us)
Sparse Core Ops, SparseCore 0:
  222.7 74.3 all-gather.1
where the time goes:
time: 408 us; the launch traced here: 402 us
  waiting for transfers between devices  202 us (50%)
  starting transfers between devices  83.3 us (20%)
  matrix products  31.1 us (8%)
  other arithmetic  23.9 us (6%)
  local copies, waits for them, and re-layouts  21.1 us (5%)
  between operations  15.3 us (4%)
  Pallas kernels  14.3 us (4%)
  blocking collectives  10.6 us (3%)
    ppermute x26, waiting for transfers between devices, permute_grid(): return lax.ppermute(block, 'kfac', route)  144 us
    ppermute x26, starting transfers between devices, permute_grid(): return lax.ppermute(block, 'kfac', route)  46.6 us
    ppermute x3, waiting for transfers between devices, pass_down(): lax.ppermute(block, 'section', [(i, i - 2) for i in range(2, sections)])  27.5 us
    dot_general x8, matrix products, dot_nt(): lax.dot_general(left, right, (((1,), (1,)), ((), ())), preferred_element_...  19.9 us
    dynamic_update_slice x20, local copies, waits for them, and re-layouts, join(): joined = lax.dynamic_update_slice(joined, part, (start, 0))  16 us
    ppermute x6, starting transfers between devices, from_row(): return lax.ppermute(block, ('section', 'kfac'), route)  14.3 us
    dot_general x10, matrix products, dot_nn(): lax.dot_general(left, right, (((1,), (0,)), ((), ())), preferred_element_...  11.2 us
    ppermute x10, waiting for transfers between devices, swap_cores(): return lax.ppermute(block, 'section', [(i, i ^ 1) for i in range(sections)])  10.8 us
  transfers between devices with their start and end apart: 52, of which 35 were waited for; matrix products, arithmetic and copies ran while one was open for 17% of the time, Pallas kernels for 1%

commit v1 on v0

--- a/solution.py
+++ b/solution.py
@@ -152,9 +152,9 @@
         out_ref[i * size : (i + 1) * size, :] = product.astype(out_ref.dtype)
 
 
-def spread(slots, left, right, height):
+def spread(slots, left, right, height, width):
     depth = left.shape[1]
-    width = right.shape[1]
+    place = right.shape[1] // width - 1
     block_count = slots.shape[0]
     streams = [
         pl.BlockSpec(
@@ -167,7 +167,7 @@
         grid_spec=pltpu.PrefetchScalarGridSpec(
             num_scalar_prefetch=1,
             grid=(block_count // 2,),
-            in_specs=streams + [pl.BlockSpec((depth, width), lambda b, slots: (0, 0))],
+            in_specs=streams + [pl.BlockSpec((depth, width), lambda b, slots: (0, place))],
             out_specs=pl.BlockSpec((2 * height, width), lambda b, slots: (b, 0)),
         ),
         out_shape=jax.ShapeDtypeStruct((block_count * height, width), BF),
@@ -273,8 +273,11 @@
                 kind = len(gathered) * stripe
                 rows = [part[kind : kind + stripe] for part in even]
                 kept, received = core_groups(rows, 0, block)
-        gathered.append(join(last, near[0], far, near[1]))
-    back_odd, proj_odd, back_even, proj_even = gathered
+        gathered.append((last, near, far))
+    back_odd, proj_odd, back_even, proj_even = [
+        join(last, near[0], [after(part, *following) for part in far], near[1])
+        for (last, near, far), following in zip(gathered, sent[1:] + [(), ()])
+    ]
     chain_weights = ((back_odd, proj_odd), (back_even, proj_even))
 
     top = top.reshape(SIDE, group_tokens, shard_width)
@@ -291,7 +294,7 @@
     targets = owners[0] + slot_numbers(owners[0])
     mine = targets == kfac_here
     block_here = jnp.sum(jnp.where(mine, jnp.arange(block_count, dtype=jnp.int32), 0))
-    left_here = left_product(block_here[None], input_inverses[0, 0], x)
+    left_here = left_product(after(block_here[None], *sent[0]), input_inverses[0, 0], x)
 
     saved = None
     for visit in range(section_count // 2):
@@ -322,8 +325,8 @@
     output = jnp.where(odd_here, shard_odd, shard_even).reshape(group_tokens, SIDE, shard_width)
     both = jnp.swapaxes(jnp.concatenate([output, right], axis=2), 0, 1)
     both = exchange(both, ROW_GROUPS).reshape(tokens, shard_width + stripe)
-    outputs, right = both[:, :shard_width], both[:, shard_width:]
-    result = spread(targets, left_all, right, block_width)
+    outputs = both[:, :shard_width]
+    result = spread(targets, left_all, both, block_width, stripe)
     return outputs.reshape(1, micro, per_micro, shard_width), result[None]
 
 

time: 408 us -> 402 us (0.985)
  starting transfers between devices: 83.3 us -> 77.6 us
    ppermute x26, starting transfers between devices: 46.6 us -> 40.6 us  [permute_grid(): return lax.ppermute(block, 'kfac', route)]
  transfers between devices with their start and end apart: 52 -> 52, of which waited for: 35 -> 36; matrix products, arithmetic and copies ran while one was open for 17% -> 17% of each run, Pallas kernels for 1% -> 1%
where the time goes in v1:
time: 402 us; the launch traced here: 396 us
  waiting for transfers between devices  205 us (51%)
  starting transfers between devices  77.6 us (19%)
  matrix products  31.1 us (8%)
  local copies, waits for them, and re-layouts  22 us (5%)
  other arithmetic  20.5 us (5%)
  between operations  15.3 us (4%)
  Pallas kernels  14.3 us (4%)
  blocking collectives  10.6 us (3%)
    ppermute x26, waiting for transfers between devices, permute_grid(): return lax.ppermute(block, 'kfac', route)  148 us
    ppermute x26, starting transfers between devices, permute_grid(): return lax.ppermute(block, 'kfac', route)  40.6 us
    ppermute x3, waiting for transfers between devices, pass_down(): lax.ppermute(block, 'section', [(i, i - 2) for i in range(2, sections)])  27.2 us
    dot_general x8, matrix products, dot_nt(): lax.dot_general(left, right, (((1,), (1,)), ((), ())), preferred_element_...  19.9 us
    ppermute x6, starting transfers between devices, from_row(): return lax.ppermute(block, ('section', 'kfac'), route)  14.3 us
    dynamic_update_slice x20, local copies, waits for them, and re-layouts, join(): joined = lax.dynamic_update_slice(joined, part, (start, 0))  13.3 us
    dot_general x10, matrix products, dot_nn(): lax.dot_general(left, right, (((1,), (0,)), ((), ())), preferred_element_...  11.3 us
    all_to_all x1, blocking collectives, exchange(): return lax.all_to_all(pieces, 'kfac', 0, 0, axis_index_groups=groups)  10.6 us
  transfers between devices with their start and end apart: 52, of which 36 were waited for; matrix products, arithmetic and copies ran while one was open for 17% of the time, Pallas kernels for 1%

profile of v1, /device:TPU:0, one launch (start us, length us, event | category | flops | bytes accessed | tf_op | source)
XLA Modules:
  0.0 396.3 jit_solution(672161640069624423)
XLA Ops:
  28.0 5.2 %all-to-all-start.1 = ((bf16[16,64,128]{2,1,0:T(8,128)(2,1)}), bf16[16,64,128]{2,1,0:T(8,128)(2,1)}, u32[]{:S(2)}, u32[]{:S(2)}) async-start(bf16[16,64,128]{2,1,0:T(8,128)(2,1)} %bitcast.10), calls=%async_computation.1 | async-start | bytes 524288 | tf_op jit(solution)/shard_map/all_to_all | solution.py:215
  33.7 8.6 %all-to-all-done.1 = bf16[16,64,128]{2,1,0:T(8,128)(2,1)} async-done(((bf16[16,64,128]{2,1,0:T(8,128)(2,1)}), bf16[16,64,128]{2,1,0:T(8,128)(2,1)}, u32[]{:S(2)}, u32[]{:S(2)}) %all-to-all-start.1) | async-done | bytes 262176 | tf_op jit(solution)/shard_map/all_to_all | solution.py:215
  71.3 8.9 %collective-permute-done.8 = bf16[256,2048]{1,0:T(8,128)(2,1)S(1)} collective-permute-done((bf16[256,2048]{1,0:T(8,128)(2,1)}, bf16[256,2048]{1,0:T(8,128)(2,1)S(1)}, u32[]{:S(2)}, u32[]{:S(2)}) %collective-permute-start.8) | collective-permute-done | bytes 1048608 | tf_op jit(solution)/shard_map/ppermute | solution.py:46
  109.4 13.6 %collective-permute-done.11 = bf16[384,2048]{1,0:T(8,128)(2,1)} collective-permute-done((bf16[384,2048]{1,0:T(8,128)(2,1)}, bf16[384,2048]{1,0:T(8,128)(2,1)}, u32[]{:S(2)}, u32[]{:S(2)}) %collective-permute-start.11) | collective-permute-done | bytes 1572896 | tf_op jit(solution)/shard_map/ppermute | solution.py:31
  148.6 10.1 %collective-permute-done.17 = bf16[384,2048]{1,0:T(8,128)(2,1)S(1)} collective-permute-done((bf16[384,2048]{1,0:T(8,128)(2,1)S(1)}, bf16[384,2048]{1,0:T(8,128)(2,1)S(1)}, u32[]{:S(2)}, u32[]{:S(2)}) %collective-permute-start.17) | collective-permute-done | bytes 1572896 | tf_op jit(solution)/shard_map/ppermute | solution.py:31
  167.8 28.3 %collective-permute-done.21 = bf16[384,2048]{1,0:T(8,128)(2,1)S(1)} collective-permute-done((bf16[384,2048]{1,0:T(8,128)(2,1)S(1)}, bf16[384,2048]{1,0:T(8,128)(2,1)S(1)}, u32[]{:S(2)}, u32[]{:S(2)}) %collective-permute-start.21) | collective-permute-done | bytes 1572896 | tf_op jit(solution)/shard_map/ppermute | solution.py:31
  209.2 5.4 %collective-permute-done.23 = bf16[64,1024]{1,0:T(8,128)(2,1)S(1)} collective-permute-done((bf16[64,1024]{1,0:T(8,128)(2,1)S(1)}, bf16[64,1024]{1,0:T(8,128)(2,1)S(1)}, u32[]{:S(2)}, u32[]{:S(2)}) %collective-permute-start.23) | collective-permute-done | bytes 131104 | tf_op jit(solution)/shard_map/ppermute | solution.py:31
  218.8 9.1 %collective-permute-done.27 = bf16[64,2048]{1,0:T(8,128)(2,1)S(1)} collective-permute-done((bf16[64,2048]{1,0:T(8,128)(2,1)S(1)}, bf16[64,2048]{1,0:T(8,128)(2,1)S(1)}, u32[]{:S(2)}, u32[]{:S(2)}) %collective-permute-start.27) | collective-permute-done | bytes 262176 | tf_op jit(solution)/shard_map/ppermute | solution.py:61
  232.4 7.7 %collective-permute-done.28 = bf16[64,1024]{1,0:T(8,128)(2,1)S(1)} collective-permute-done((bf16[64,1024]{1,0:T(8,128)(2,1)S(1)}, bf16[64,1024]{1,0:T(8,128)(2,1)S(1)}, u32[]{:S(2)}, u32[]{:S(2)}) %collective-permute-start.28) | collective-permute-done | bytes 131104 | tf_op jit(solution)/shard_map/ppermute | solution.py:31
  240.4 6.0 %collective-permute-done.29 = bf16[64,1024]{1,0:T(8,128)(2,1)S(1)} collective-permute-done((bf16[64,1024]{1,0:T(8,128)(2,1)S(1)}, bf16[64,1024]{1,0:T(8,128)(2,1)S(1)}, u32[]{:S(2)}, u32[]{:S(2)}) %collective-permute-start.29) | collective-permute-done | bytes 131104 | tf_op jit(solution)/shard_map/ppermute | solution.py:31
  250.4 10.1 %collective-permute-start.31 = (bf16[64,1024]{1,0:T(8,128)(2,1)S(1)}, bf16[64,1024]{1,0:T(8,128)(2,1)S(1)}, u32[]{:S(2)}, u32[]{:S(2)}) collective-permute-start(bf16[64,1024]{1,0:T(8,128)(2,1)S(1)} %convolution_convert_fusion.4), channel_id=1, source_target_pairs={{4,0},{5,1},{6,2},{7,3},{0,4},{1,5},{2,6},{3,7},{12,8},{13,9},{14,... | collective-permute-start | bytes 393224 | tf_op jit(solution)/shard_map/ppermute | solution.py:31
  260.5 8.9 %collective-permute-done.31 = bf16[64,1024]{1,0:T(8,128)(2,1)S(1)} collective-permute-done((bf16[64,1024]{1,0:T(8,128)(2,1)S(1)}, bf16[64,1024]{1,0:T(8,128)(2,1)S(1)}, u32[]{:S(2)}, u32[]{:S(2)}) %collective-permute-start.31) | collective-permute-done | bytes 131104 | tf_op jit(solution)/shard_map/ppermute | solution.py:31
  269.7 9.6 %collective-permute-done.32 = bf16[64,1024]{1,0:T(8,128)(2,1)S(1)} collective-permute-done((bf16[64,1024]{1,0:T(8,128)(2,1)S(1)}, bf16[64,1024]{1,0:T(8,128)(2,1)S(1)}, u32[]{:S(2)}, u32[]{:S(2)}) %collective-permute-start.32) | collective-permute-done | bytes 131104 | tf_op jit(solution)/shard_map/ppermute | solution.py:31
  283.2 9.1 %collective-permute-done.34 = bf16[64,2048]{1,0:T(8,128)(2,1)S(1)} collective-permute-done((bf16[64,2048]{1,0:T(8,128)(2,1)S(1)}, bf16[64,2048]{1,0:T(8,128)(2,1)S(1)}, u32[]{:S(2)}, u32[]{:S(2)}) %collective-permute-start.34) | collective-permute-done | bytes 262176 | tf_op jit(solution)/shard_map/ppermute | solution.py:61
  296.0 5.0 %collective-permute-done.35 = bf16[64,1024]{1,0:T(8,128)(2,1)S(1)} collective-permute-done((bf16[64,1024]{1,0:T(8,128)(2,1)S(1)}, bf16[64,1024]{1,0:T(8,128)(2,1)S(1)}, u32[]{:S(2)}, u32[]{:S(2)}) %collective-permute-start.35) | collective-permute-done | bytes 131104 | tf_op jit(solution)/shard_map/ppermute | solution.py:31
  301.5 5.8 %collective-permute-done.36 = bf16[64,1024]{1,0:T(8,128)(2,1)S(1)} collective-permute-done((bf16[64,1024]{1,0:T(8,128)(2,1)S(1)}, bf16[64,1024]{1,0:T(8,128)(2,1)S(1)}, u32[]{:S(2)}, u32[]{:S(2)}) %collective-permute-start.36) | collective-permute-done | bytes 131104 | tf_op jit(solution)/shard_map/ppermute | solution.py:31
  311.3 5.5 %collective-permute-done.38 = bf16[64,1024]{1,0:T(8,128)(2,1)S(1)} collective-permute-done((bf16[64,1024]{1,0:T(8,128)(2,1)S(1)}, bf16[64,1024]{1,0:T(8,128)(2,1)S(1)}, u32[]{:S(2)}, u32[]{:S(2)}) %collective-permute-start.38) | collective-permute-done | bytes 131104 | tf_op jit(solution)/shard_map/ppermute | solution.py:31
  317.4 5.8 %collective-permute-done.39 = bf16[64,1024]{1,0:T(8,128)(2,1)S(1)} collective-permute-done((bf16[64,1024]{1,0:T(8,128)(2,1)S(1)}, bf16[64,1024]{1,0:T(8,128)(2,1)S(1)}, u32[]{:S(2)}, u32[]{:S(2)}) %collective-permute-start.39) | collective-permute-done | bytes 131104 | tf_op jit(solution)/shard_map/ppermute | solution.py:31
  327.0 8.9 %collective-permute-done.41 = bf16[64,2048]{1,0:T(8,128)(2,1)S(1)} collective-permute-done((bf16[64,2048]{1,0:T(8,128)(2,1)S(1)}, bf16[64,2048]{1,0:T(8,128)(2,1)S(1)}, u32[]{:S(2)}, u32[]{:S(2)}) %collective-permute-start.41) | collective-permute-done | bytes 262176 | tf_op jit(solution)/shard_map/ppermute | solution.py:61
  339.7 5.0 %collective-permute-done.42 = bf16[64,1024]{1,0:T(8,128)(2,1)S(1)} collective-permute-done((bf16[64,1024]{1,0:T(8,128)(2,1)S(1)}, bf16[64,1024]{1,0:T(8,128)(2,1)S(1)}, u32[]{:S(2)}, u32[]{:S(2)}) %collective-permute-start.42) | collective-permute-done | bytes 131104 | tf_op jit(solution)/shard_map/ppermute | solution.py:31
  345.1 5.8 %collective-permute-done.43 = bf16[64,1024]{1,0:T(8,128)(2,1)S(1)} collective-permute-done((bf16[64,1024]{1,0:T(8,128)(2,1)S(1)}, bf16[64,1024]{1,0:T(8,128)(2,1)S(1)}, u32[]{:S(2)}, u32[]{:S(2)}) %collective-permute-start.43) | collective-permute-done | bytes 131104 | tf_op jit(solution)/shard_map/ppermute | solution.py:31
  355.1 5.6 %collective-permute-done.45 = bf16[64,1024]{1,0:T(8,128)(2,1)} collective-permute-done((bf16[64,1024]{1,0:T(8,128)(2,1)S(1)}, bf16[64,1024]{1,0:T(8,128)(2,1)}, u32[]{:S(2)}, u32[]{:S(2)}) %collective-permute-start.45) | collective-permute-done | bytes 131104 | tf_op jit(solution)/shard_map/ppermute | solution.py:31
  372.2 10.6 %all_to_all.15 = bf16[4,64,640]{2,1,0:T(8,128)(2,1)S(1)} all-to-all(bf16[4,64,640]{2,1,0:T(8,128)(2,1)S(1)} %maximum_bitcast_fusion), channel_id=1, replica_groups={{0,1,2,3},{4,5,6,7},{8,9,10,11},{12,13,14,15},{16,17,18,19},{20,21,22,2..., dimensions={0} | all-to-all | bytes 655360 | tf_op jit(solution)/shard_map/all_to_all | solution.py:72
  383.6 5.6 %shard_map.88 = bf16[8192,128]{1,0:T(8,128)(2,1)} custom-call(s32[8]{0:T(128)} %get-tuple-element.56.slots_ref, bf16[16384,256]{1,0:T(8,128)(2,1)} %all-gather.2.cloned.1.call-done.refs_0_.refs_1_.refs_2_.refs_3_, bf16[16384,256]{1,0:T(8,128)(2,1)} %all-gather.2.cloned.1.call-done.refs_0_.refs_1_.refs_2_.refs_3_, ...), custom_call_target="tpu_custom_call" | custom-call | flops 536870912 | bytes 6291456 | tf_op jit(solution)/shard_map/pallas_call | solution.py:165
  (231 shorter events, 176.9 us)
Async XLA Ops:
  12.0 30.2 %collective-permute-start.2 = (bf16[256,2048]{1,0:T(8,128)(2,1)}, bf16[256,2048]{1,0:T(8,128)(2,1)S(1)}, u32[]{:S(2)}, u32[]{:S(2)}) collective-permute-start(bf16[256,2048]{1,0:T(8,128)(2,1)} %get-tuple-element.35), channel_id=1, source_target_pairs={{28,16},{29,17},{30,18},{31,19},{16,20},{17,21},{18,22},{19,23},{2... | collective-permute-start | bytes 3145736 | tf_op jit(solution)/shard_map/ppermute | solution.py:46
  12.8 29.4 %collective-permute-start.1 = (bf16[256,2048]{1,0:T(8,128)(2,1)}, bf16[256,2048]{1,0:T(8,128)(2,1)}, u32[]{:S(2)}, u32[]{:S(2)}) collective-permute-start(bf16[256,2048]{1,0:T(8,128)(2,1)} %get-tuple-element.34), channel_id=1, source_target_pairs={{24,16},{25,17},{26,18},{27,19},{28,20},{29,21},{30,22},{31,23},{1... | collective-permute-start | bytes 3145736 | tf_op jit(solution)/shard_map/ppermute | solution.py:46
  14.5 27.7 %collective-permute-start = (bf16[256,2048]{1,0:T(8,128)(2,1)}, bf16[256,2048]{1,0:T(8,128)(2,1)}, u32[]{:S(2)}, u32[]{:S(2)}) collective-permute-start(bf16[256,2048]{1,0:T(8,128)(2,1)} %get-tuple-element.33), channel_id=1, source_target_pairs={{20,16},{21,17},{22,18},{23,19},{24,20},{25,21},{26,22},{27,23},{2... | collective-permute-start | bytes 3145736 | tf_op jit(solution)/shard_map/ppermute | solution.py:46
  16.2 11.1 %all-to-all-start = ((bf16[4,64,512]{2,1,0:T(8,128)(2,1)}), bf16[4,64,512]{2,1,0:T(8,128)(2,1)S(1)}, u32[]{:S(2)}, u32[]{:S(2)}) async-start(bf16[4,64,512]{2,1,0:T(8,128)(2,1)} %bitcast), calls=%async_computation | async-start | bytes 524288 | tf_op jit(solution)/shard_map/all_to_all | solution.py:72
  28.0 14.2 %all-to-all-start.1 = ((bf16[16,64,128]{2,1,0:T(8,128)(2,1)}), bf16[16,64,128]{2,1,0:T(8,128)(2,1)}, u32[]{:S(2)}, u32[]{:S(2)}) async-start(bf16[16,64,128]{2,1,0:T(8,128)(2,1)} %bitcast.10), calls=%async_computation.1 | async-start | bytes 524288 | tf_op jit(solution)/shard_map/all_to_all | solution.py:215
  33.2 350.3 %all-gather.2.cloned.1.call-start = ((), (), s32[]{:S(2)}) async-start(), calls=%async_computation.3 | async-start | bytes 8912896 | tf_op jit(solution)/shard_map/all_gather | solution.py:316
  45.5 13.9 %collective-permute-start.3 = (bf16[256,2048]{1,0:T(8,128)(2,1)}, bf16[256,2048]{1,0:T(8,128)(2,1)}, u32[]{:S(2)}, u32[]{:S(2)}) collective-permute-start(bf16[256,2048]{1,0:T(8,128)(2,1)} %pad_maximum_fusion.6), channel_id=1, source_target_pairs={{16,0},{48,32},{80,64},{112,96},{17,1},{49,33},{81,65},{113,97},{1... | collective-permute-start | bytes 3145736 | tf_op jit(solution)/shard_map/ppermute | solution.py:51
  47.9 18.0 %collective-permute-start.6 = (bf16[256,2048]{1,0:T(8,128)(2,1)}, bf16[256,2048]{1,0:T(8,128)(2,1)S(1)}, u32[]{:S(2)}, u32[]{:S(2)}) collective-permute-start(bf16[256,2048]{1,0:T(8,128)(2,1)} %get-tuple-element.33), channel_id=1, source_target_pairs={{4,0},{5,1},{6,2},{7,3},{8,4},{9,5},{10,6},{11,7},{12,8},{13,9},{1... | collective-permute-start | bytes 3145736 | tf_op jit(solution)/shard_map/ppermute | solution.py:46
  50.6 20.7 %collective-permute-start.7 = (bf16[256,2048]{1,0:T(8,128)(2,1)}, bf16[256,2048]{1,0:T(8,128)(2,1)S(1)}, u32[]{:S(2)}, u32[]{:S(2)}) collective-permute-start(bf16[256,2048]{1,0:T(8,128)(2,1)} %get-tuple-element.34), channel_id=1, source_target_pairs={{8,0},{9,1},{10,2},{11,3},{12,4},{13,5},{14,6},{15,7},{0,8},{1,9},... | collective-permute-start | bytes 3145736 | tf_op jit(solution)/shard_map/ppermute | solution.py:46
  54.7 25.5 %collective-permute-start.8 = (bf16[256,2048]{1,0:T(8,128)(2,1)}, bf16[256,2048]{1,0:T(8,128)(2,1)S(1)}, u32[]{:S(2)}, u32[]{:S(2)}) collective-permute-start(bf16[256,2048]{1,0:T(8,128)(2,1)} %get-tuple-element.35), channel_id=1, source_target_pairs={{12,0},{13,1},{14,2},{15,3},{0,4},{1,5},{2,6},{3,7},{4,8},{5,9},{6... | collective-permute-start | bytes 3145736 | tf_op jit(solution)/shard_map/ppermute | solution.py:46
  61.1 22.6 %collective-permute-start.5 = (bf16[256,2048]{1,0:T(8,128)(2,1)S(1)}, bf16[256,2048]{1,0:T(8,128)(2,1)S(1)}, u32[]{:S(2)}, u32[]{:S(2)}) collective-permute-start(bf16[256,2048]{1,0:T(8,128)(2,1)S(1)} %maximum_select_fusion), channel_id=1, source_target_pairs={{3,0},{0,1},{1,2},{2,3},{7,4},{4,5},{5,6},{6,7},{11,8},{8,9},{9,10... | collective-permute-start | bytes 3145736 | tf_op jit(solution)/shard_map/ppermute | solution.py:31
  61.2 22.5 %collective-permute-start.4 = (bf16[256,2048]{1,0:T(8,128)(2,1)S(1)}, bf16[256,2048]{1,0:T(8,128)(2,1)S(1)}, u32[]{:S(2)}, u32[]{:S(2)}) collective-permute-start(bf16[256,2048]{1,0:T(8,128)(2,1)S(1)} %maximum_select_fusion), channel_id=1, source_target_pairs={{1,0},{2,1},{3,2},{0,3},{5,4},{6,5},{7,6},{4,7},{9,8},{10,9},{11,1... | collective-permute-start | bytes 3145736 | tf_op jit(solution)/shard_map/ppermute | solution.py:31
  65.9 17.8 %collective-permute-start.9 = (bf16[256,2048]{1,0:T(8,128)(2,1)S(1)}, bf16[256,2048]{1,0:T(8,128)(2,1)S(1)}, u32[]{:S(2)}, u32[]{:S(2)}) collective-permute-start(bf16[256,2048]{1,0:T(8,128)(2,1)S(1)} %pad_maximum_fusion.8), channel_id=1, source_target_pairs={{16,0},{48,32},{80,64},{112,96},{17,1},{49,33},{81,65},{113,97},{1... | collective-permute-start | bytes 3145736 | tf_op jit(solution)/shard_map/ppermute | solution.py:51
  85.2 19.1 %collective-permute-start.13 = (bf16[256,2048]{1,0:T(8,128)(2,1)}, bf16[256,2048]{1,0:T(8,128)(2,1)}, u32[]{:S(2)}, u32[]{:S(2)}) collective-permute-start(bf16[256,2048]{1,0:T(8,128)(2,1)} %pad_maximum_fusion.10), channel_id=1, source_target_pairs={{0,16},{32,48},{64,80},{96,112},{1,17},{33,49},{65,81},{97,113},{2... | collective-permute-start | bytes 3145736 | tf_op jit(solution)/shard_map/ppermute | solution.py:51
  89.7 33.3 %collective-permute-start.11 = (bf16[384,2048]{1,0:T(8,128)(2,1)}, bf16[384,2048]{1,0:T(8,128)(2,1)}, u32[]{:S(2)}, u32[]{:S(2)}) collective-permute-start(bf16[384,2048]{1,0:T(8,128)(2,1)} %get-tuple-element.87), channel_id=1, source_target_pairs={{3,0},{0,1},{1,2},{2,3},{7,4},{4,5},{5,6},{6,7},{11,8},{8,9},{9,10... | collective-permute-start | bytes 4718600 | tf_op jit(solution)/shard_map/ppermute | solution.py:31
  91.2 32.5 %collective-permute-start.10 = (bf16[384,2048]{1,0:T(8,128)(2,1)}, bf16[384,2048]{1,0:T(8,128)(2,1)}, u32[]{:S(2)}, u32[]{:S(2)}) collective-permute-start(bf16[384,2048]{1,0:T(8,128)(2,1)} %get-tuple-element.88), channel_id=1, source_target_pairs={{1,0},{2,1},{3,2},{0,3},{5,4},{6,5},{7,6},{4,7},{9,8},{10,9},{11,1... | collective-permute-start | bytes 4718600 | tf_op jit(solution)/shard_map/ppermute | solution.py:31
  106.6 41.4 %collective-permute-start.18 = (bf16[256,2048]{1,0:T(8,128)(2,1)S(1)}, bf16[256,2048]{1,0:T(8,128)(2,1)S(1)}, u32[]{:S(2)}, u32[]{:S(2)}) collective-permute-start(bf16[256,2048]{1,0:T(8,128)(2,1)S(1)} %pad_maximum_fusion.12), channel_id=1, source_target_pairs={{0,16},{32,48},{64,80},{96,112},{1,17},{33,49},{65,81},{97,113},{2... | collective-permute-start | bytes 3145736 | tf_op jit(solution)/shard_map/ppermute | solution.py:51
  125.8 32.9 %collective-permute-start.17 = (bf16[384,2048]{1,0:T(8,128)(2,1)S(1)}, bf16[384,2048]{1,0:T(8,128)(2,1)S(1)}, u32[]{:S(2)}, u32[]{:S(2)}) collective-permute-start(bf16[384,2048]{1,0:T(8,128)(2,1)S(1)} %get-tuple-element.85), channel_id=1, source_target_pairs={{3,0},{0,1},{1,2},{2,3},{7,4},{4,5},{5,6},{6,7},{11,8},{8,9},{9,10... | collective-permute-start | bytes 4718600 | tf_op jit(solution)/shard_map/ppermute | solution.py:31
  127.6 33.8 %collective-permute-start.16 = (bf16[384,2048]{1,0:T(8,128)(2,1)S(1)}, bf16[384,2048]{1,0:T(8,128)(2,1)S(1)}, u32[]{:S(2)}, u32[]{:S(2)}) collective-permute-start(bf16[384,2048]{1,0:T(8,128)(2,1)S(1)} %get-tuple-element.86), channel_id=1, source_target_pairs={{1,0},{2,1},{3,2},{0,3},{5,4},{6,5},{7,6},{4,7},{9,8},{10,9},{11,1... | collective-permute-start | bytes 4718600 | tf_op jit(solution)/shard_map/ppermute | solution.py:31
  161.8 34.3 %collective-permute-start.21 = (bf16[384,2048]{1,0:T(8,128)(2,1)S(1)}, bf16[384,2048]{1,0:T(8,128)(2,1)S(1)}, u32[]{:S(2)}, u32[]{:S(2)}) collective-permute-start(bf16[384,2048]{1,0:T(8,128)(2,1)S(1)} %get-tuple-element.81), channel_id=1, source_target_pairs={{3,0},{0,1},{1,2},{2,3},{7,4},{4,5},{5,6},{6,7},{11,8},{8,9},{9,10... | collective-permute-start | bytes 4718600 | tf_op jit(solution)/shard_map/ppermute | solution.py:31
  162.5 34.6 %collective-permute-start.20 = (bf16[384,2048]{1,0:T(8,128)(2,1)S(1)}, bf16[384,2048]{1,0:T(8,128)(2,1)S(1)}, u32[]{:S(2)}, u32[]{:S(2)}) collective-permute-start(bf16[384,2048]{1,0:T(8,128)(2,1)S(1)} %get-tuple-element.82), channel_id=1, source_target_pairs={{1,0},{2,1},{3,2},{0,3},{5,4},{6,5},{7,6},{4,7},{9,8},{10,9},{11,1... | collective-permute-start | bytes 4718600 | tf_op jit(solution)/shard_map/ppermute | solution.py:31
  196.1 13.0 %collective-permute-start.25 = (bf16[128,2048]{1,0:T(8,128)(2,1)S(1)}, bf16[128,2048]{1,0:T(8,128)(2,1)S(1)}, u32[]{:S(2)}, u32[]{:S(2)}) collective-permute-start(bf16[128,2048]{1,0:T(8,128)(2,1)S(1)} %get-tuple-element.70), channel_id=1, source_target_pairs={{3,0},{0,1},{1,2},{2,3},{7,4},{4,5},{5,6},{6,7},{11,8},{8,9},{9,10... | collective-permute-start | bytes 1572872 | tf_op jit(solution)/shard_map/ppermute | solution.py:31
  197.2 11.9 %collective-permute-start.24 = (bf16[128,2048]{1,0:T(8,128)(2,1)S(1)}, bf16[128,2048]{1,0:T(8,128)(2,1)S(1)}, u32[]{:S(2)}, u32[]{:S(2)}) collective-permute-start(bf16[128,2048]{1,0:T(8,128)(2,1)S(1)} %get-tuple-element.72), channel_id=1, source_target_pairs={{1,0},{2,1},{3,2},{0,3},{5,4},{6,5},{7,6},{4,7},{9,8},{10,9},{11,1... | collective-permute-start | bytes 1572872 | tf_op jit(solution)/shard_map/ppermute | solution.py:31
  250.4 18.9 %collective-permute-start.31 = (bf16[64,1024]{1,0:T(8,128)(2,1)S(1)}, bf16[64,1024]{1,0:T(8,128)(2,1)S(1)}, u32[]{:S(2)}, u32[]{:S(2)}) collective-permute-start(bf16[64,1024]{1,0:T(8,128)(2,1)S(1)} %convolution_convert_fusion.4), channel_id=1, source_target_pairs={{4,0},{5,1},{6,2},{7,3},{0,4},{1,5},{2,6},{3,7},{12,8},{13,9},{14,... | collective-permute-start | bytes 393224 | tf_op jit(solution)/shard_map/ppermute | solution.py:31
  (48 other events, 383.9 us)
Sparse Core Ops, SparseCore 0:
  217.3 73.4 all-gather.1
